TPU v7x, 32 devices: a whole 2x2x4 slice. The times are simulated.
32 devices in a mesh: gx: 4 (over y, x), gy: 8 (over z, core).
Axes of the slice: x: 2, y: 2, z: 4, core: 2. Of those that a mesh axis runs over, the one named last changes fastest.
Arguments:
- tgt: bfloat16 [32, 1024, 512], P(('gx', 'gy')), may hold values from -4 to 4
- memory: bfloat16 [32, 1024, 512], P(('gx', 'gy')), may hold values from -4 to 4
- cotangent: bfloat16 [32, 1024, 512], P(('gx', 'gy')), may hold values from -4 to 4
- tgt_lengths: int32 [32, 48], P(('gx', 'gy')), may hold values from 1 to 512, 1024 in all within a row
- src_segments: int32 [32, 1024], P(('gx', 'gy')), may hold values from 0 to 47, never falling along the last dimension, each value on 1 to 512 neighbouring positions
- attn_w: float32 [8, 512, 512], P(None, ('gx', 'gy')), may hold values from -1.2374369 to 1.2374369
- ffn_in: float32 [512, 2048], P(('gx', 'gy')), may hold values from -0.30935922 to 0.30935922
- ffn_out: float32 [2048, 512], P(('gx', 'gy')), may hold values from -0.15467961 to 0.15467961
- norm_params: float32 [6, 512], P(None, ('gx', 'gy')), may hold values from -2.5 to 2.5, as said below
- attn_moments: float32 [2, 8, 512, 512], P(None, None, ('gx', 'gy')), may hold values from -347.55713 to 11796.48, as said below
- in_moments: float32 [2, 512, 2048], P(None, ('gx', 'gy')), may hold values from -289.63094 to 8192, as said below
- out_moments: float32 [2, 2048, 512], P(None, ('gx', 'gy')), may hold values from -695.11425 to 47185.92, as said below
- norm_moments: float32 [2, 6, 512], P(None, None, ('gx', 'gy')), may hold values from -1158.5238 to 131072, as said below
Outputs:
- layer_out: bfloat16 [32, 1024, 512], P(('gx', 'gy'))
- tgt_grad: bfloat16 [32, 1024, 512], P(('gx', 'gy'))
- mem_grad: bfloat16 [32, 1024, 512], P(('gx', 'gy'))
- attn_new: float32 [8, 512, 512], P(None, ('gx', 'gy'))
- in_new: float32 [512, 2048], P(('gx', 'gy'))
- out_new: float32 [2048, 512], P(('gx', 'gy'))
- norm_new: float32 [6, 512], P(None, ('gx', 'gy'))
- attn_first_new: float32 [8, 512, 512], P(None, ('gx', 'gy'))
- attn_second_new: float32 [8, 512, 512], P(None, ('gx', 'gy'))
- in_first_new: float32 [512, 2048], P(('gx', 'gy'))
- in_second_new: float32 [512, 2048], P(('gx', 'gy'))
- out_first_new: float32 [2048, 512], P(('gx', 'gy'))
- out_second_new: float32 [2048, 512], P(('gx', 'gy'))
- norm_first_new: float32 [6, 512], P(None, ('gx', 'gy'))
- norm_second_new: float32 [6, 512], P(None, ('gx', 'gy'))
- attn_copy: bfloat16 [8, 512, 512], P(None, ('gx', 'gy'))
- in_copy: bfloat16 [512, 2048], P(('gx', 'gy'))
- out_copy: bfloat16 [2048, 512], P(('gx', 'gy'))
- norm_copy: bfloat16 [6, 512], P(None, ('gx', 'gy'))
- norms: float32 [2, 16], replicated
Inputs may be any that keep to these rules, and one draw needn't show every extreme that they name: `tgt_lengths`: each row's 48 lengths sum to 1024; every row has one length equal to 512. `src_segments`: in each row the numbers never fall and take every value from 0 to 47, each for at most 512 positions; target sentence s of a row is translated from its memory rows numbered s. `norm_params`: gains are positive. `attn_moments`: element 0 holds first moments, element 1 positive second moments. `in_moments`: element 0 holds first moments, element 1 positive second moments. `out_moments`: element 0 holds first moments, element 1 positive second moments. `norm_moments`: element 0 holds first moments, element 1 positive second moments.
All inputs are finite; a program needn't handle non-finite values.
Results may differ from a plain program's by a relative error of at most 0.03.
The roundings to bfloat16 on the way count: a program that leaves them out, or rounds other values in their place, can miss the bound.
Values may be sent and summed in bfloat16 or wider, within the bound.
A program may use at most 192 MiB of HBM per device.

v0:
```python
import jax
import jax.numpy as jnp
from jax import lax
from jax.sharding import PartitionSpec as P

HEAD_DIM = 64
STEP = 5


beta_first = 0.5
beta_second = 0.5
learn_rate = 0.5
decay_rate = 0.01
norm_eps = 1e-05
adam_eps = 1e-06
masked_value = -1000000000.0


def segment_ids(lengths, count):
    ends = jnp.cumsum(lengths)
    places = jnp.arange(count, dtype=jnp.int32)
    return jnp.sum((ends[None, :] <= places[:, None]).astype(jnp.int32), axis=1)


def layer_norm(values, gain_row, bias_row):
    average = jnp.mean(values, axis=-1, keepdims=True)
    centred = values - average
    spread = jnp.mean(centred * centred, axis=-1, keepdims=True)
    inverse = lax.rsqrt(spread + norm_eps)
    normed = centred * inverse
    return (normed * gain_row + bias_row, normed, inverse)


def norm_back(gradient, normed, inverse, gain_row):
    scaled = gradient * gain_row
    first_mean = jnp.mean(scaled, axis=-1, keepdims=True)
    second_mean = jnp.mean(scaled * normed, axis=-1, keepdims=True)
    return (
        inverse * (scaled - first_mean - normed * second_mean),
        jnp.sum(gradient * normed, axis=0),
        jnp.sum(gradient, axis=0),
    )


def allowed_mask(seg_query, seg_key, first_row, causal):
    allowed = seg_query[:, None] == seg_key[None, :]
    if causal:
        row_places = first_row + jnp.arange(seg_query.shape[0], dtype=jnp.int32)
        key_places = jnp.arange(seg_key.shape[0], dtype=jnp.int32)
        allowed = jnp.logical_and(allowed, row_places[:, None] >= key_places[None, :])
    return allowed


def block_logits(query_block, key_heads, allowed):
    raw_scores = jnp.einsum(
        "qhd,khd->hqk", query_block, key_heads, preferred_element_type=jnp.float32
    )
    return jnp.where(allowed[None], raw_scores * HEAD_DIM ** (-0.5), masked_value)


def attend_row(queries, key_rows, value_rows, seg_query, seg_key, causal):
    length = queries.shape[0]
    block_rows = min(512, length)
    key_heads = key_rows.reshape(key_rows.shape[0], -1, HEAD_DIM)
    value_heads = value_rows.reshape(value_rows.shape[0], -1, HEAD_DIM)

    def one_block(block_index):
        first_row = block_index * block_rows
        query_block = lax.dynamic_slice_in_dim(queries, first_row, block_rows, 0).reshape(
            block_rows, -1, HEAD_DIM
        )
        seg_block = lax.dynamic_slice_in_dim(seg_query, first_row, block_rows, 0)
        logits = block_logits(
            query_block, key_heads, allowed_mask(seg_block, seg_key, first_row, causal)
        )
        row_max = jnp.max(logits, axis=-1, keepdims=True)
        exponent = jnp.exp(logits - row_max)
        row_sum = jnp.sum(exponent, axis=-1, keepdims=True)
        probability = (exponent / row_sum).astype(jnp.bfloat16)
        mixture = jnp.einsum(
            "hqk,khd->qhd", probability, value_heads, preferred_element_type=jnp.float32
        )
        return (mixture.reshape(block_rows, -1).astype(jnp.bfloat16), row_max + jnp.log(row_sum))

    mixture, log_sums = lax.map(one_block, jnp.arange(length // block_rows))
    return (mixture.reshape(length, -1), log_sums)


def attend_row_back(
    queries, key_rows, value_rows, grad_mixture, log_sums, seg_query, seg_key, causal
):
    length = queries.shape[0]
    block_rows = min(512, length)
    key_heads = key_rows.reshape(key_rows.shape[0], -1, HEAD_DIM)
    value_heads = value_rows.reshape(value_rows.shape[0], -1, HEAD_DIM)

    def one_block(carry, block_index):
        grad_keys, grad_values = carry
        first_row = block_index * block_rows
        query_block = lax.dynamic_slice_in_dim(queries, first_row, block_rows, 0).reshape(
            block_rows, -1, HEAD_DIM
        )
        grad_block = lax.dynamic_slice_in_dim(grad_mixture, first_row, block_rows, 0).reshape(
            block_rows, -1, HEAD_DIM
        )
        seg_block = lax.dynamic_slice_in_dim(seg_query, first_row, block_rows, 0)
        logits = block_logits(
            query_block, key_heads, allowed_mask(seg_block, seg_key, first_row, causal)
        )
        probability = jnp.exp(logits - log_sums[block_index])
        grad_prob = jnp.einsum(
            "qhd,khd->hqk", grad_block, value_heads, preferred_element_type=jnp.float32
        )
        row_dot = jnp.sum(probability * grad_prob, axis=-1, keepdims=True)
        grad_score = (probability * (grad_prob - row_dot) * HEAD_DIM ** (-0.5)).astype(jnp.bfloat16)
        grad_query = jnp.einsum(
            "hqk,khd->qhd", grad_score, key_heads, preferred_element_type=jnp.float32
        )
        grad_keys = grad_keys + jnp.einsum(
            "hqk,qhd->khd", grad_score, query_block, preferred_element_type=jnp.float32
        )
        grad_values = grad_values + jnp.einsum(
            "hqk,qhd->khd",
            probability.astype(jnp.bfloat16),
            grad_block,
            preferred_element_type=jnp.float32,
        )
        return ((grad_keys, grad_values), grad_query.reshape(block_rows, -1).astype(jnp.bfloat16))

    zero_heads = jnp.zeros(key_heads.shape, jnp.float32)
    (grad_keys, grad_values), grad_queries = lax.scan(
        one_block, (zero_heads, zero_heads), jnp.arange(length // block_rows)
    )
    key_count = key_rows.shape[0]
    return (
        grad_queries.reshape(length, -1),
        grad_keys.reshape(key_count, -1).astype(jnp.bfloat16),
        grad_values.reshape(key_count, -1).astype(jnp.bfloat16),
    )


def attend_rows(queries, key_rows, value_rows, seg_query, seg_key, causal):

    def per_row(row_items):
        return attend_row(
            row_items[0], row_items[1], row_items[2], row_items[3], row_items[4], causal
        )

    return lax.map(per_row, (queries, key_rows, value_rows, seg_query, seg_key))


def attend_rows_back(
    queries, key_rows, value_rows, grad_mixture, log_sums, seg_query, seg_key, causal
):

    def per_row(row_items):
        return attend_row_back(
            row_items[0],
            row_items[1],
            row_items[2],
            row_items[3],
            row_items[4],
            row_items[5],
            row_items[6],
            causal,
        )

    return lax.map(
        per_row, (queries, key_rows, value_rows, grad_mixture, log_sums, seg_query, seg_key)
    )


def layer_forward(tgt, memory, weights, seg_tgt, seg_src):
    attn_full, inner_full, outer_full, norm_full = weights
    row_count, length, model_width = tgt.shape
    tokens_flat = tgt.reshape(-1, model_width)
    memory_flat = memory.reshape(-1, model_width)
    gain_rows = norm_full.astype(jnp.float32)
    self_proj = jnp.einsum(
        "nd,jde->jne", tokens_flat, attn_full[0:3], preferred_element_type=jnp.float32
    ).astype(jnp.bfloat16)
    shaped_self = self_proj.reshape(3, row_count, length, model_width)
    self_mix, self_lse = attend_rows(
        shaped_self[0], shaped_self[1], shaped_self[2], seg_tgt, seg_tgt, True
    )
    self_mix = self_mix.reshape(-1, model_width)
    first_sum = tokens_flat.astype(jnp.float32) + jnp.dot(
        self_mix, attn_full[3], preferred_element_type=jnp.float32
    )
    first_norm, first_normed, first_inverse = layer_norm(first_sum, gain_rows[0], gain_rows[1])
    first_low = first_norm.astype(jnp.bfloat16)
    cross_query = jnp.dot(first_low, attn_full[4], preferred_element_type=jnp.float32).astype(
        jnp.bfloat16
    )
    cross_kv = jnp.einsum(
        "md,jde->jme", memory_flat, attn_full[5:7], preferred_element_type=jnp.float32
    ).astype(jnp.bfloat16)
    shaped_kv = cross_kv.reshape(2, row_count, -1, model_width)
    cross_mix, cross_lse = attend_rows(
        cross_query.reshape(row_count, length, model_width),
        shaped_kv[0],
        shaped_kv[1],
        seg_tgt,
        seg_src,
        False,
    )
    cross_mix = cross_mix.reshape(-1, model_width)
    second_sum = first_norm + jnp.dot(cross_mix, attn_full[7], preferred_element_type=jnp.float32)
    second_norm, second_normed, second_inverse = layer_norm(second_sum, gain_rows[2], gain_rows[3])
    second_low = second_norm.astype(jnp.bfloat16)
    inner_pre = jnp.dot(second_low, inner_full, preferred_element_type=jnp.float32)
    activation = jax.nn.silu(inner_pre).astype(jnp.bfloat16)
    third_sum = second_norm + jnp.dot(activation, outer_full, preferred_element_type=jnp.float32)
    final_norm, third_normed, third_inverse = layer_norm(third_sum, gain_rows[4], gain_rows[5])
    saved = (
        self_proj,
        self_mix,
        self_lse,
        first_normed,
        first_inverse,
        first_low,
        cross_query,
        cross_kv,
        cross_mix,
        cross_lse,
        second_normed,
        second_inverse,
        second_low,
        inner_pre,
        activation,
        third_normed,
        third_inverse,
    )
    return (final_norm, saved)


def layer_backward(cotangent, tgt, memory, weights, seg_tgt, seg_src, saved, ffn_ready):
    attn_full, inner_full, outer_full, norm_full = weights
    (
        self_proj,
        self_mix,
        self_lse,
        first_normed,
        first_inverse,
        first_low,
        cross_query,
        cross_kv,
        cross_mix,
        cross_lse,
        second_normed,
        second_inverse,
        second_low,
        inner_pre,
        activation,
        third_normed,
        third_inverse,
    ) = saved
    row_count, length, model_width = tgt.shape
    tokens_flat = tgt.reshape(-1, model_width)
    memory_flat = memory.reshape(-1, model_width)
    gain_rows = norm_full.astype(jnp.float32)
    out_grad = cotangent.reshape(-1, model_width).astype(jnp.float32)
    third_grad, gain_three, bias_three = norm_back(
        out_grad, third_normed, third_inverse, gain_rows[4]
    )
    third_low = third_grad.astype(jnp.bfloat16)
    grad_outer = jnp.einsum("nf,nd->fd", activation, third_low, preferred_element_type=jnp.float32)
    act_grad = jnp.einsum("nd,fd->nf", third_low, outer_full, preferred_element_type=jnp.float32)
    sigmoid_pre = jax.nn.sigmoid(inner_pre)
    pre_grad = (act_grad * sigmoid_pre * (1.0 + inner_pre * (1.0 - sigmoid_pre))).astype(
        jnp.bfloat16
    )
    grad_inner = jnp.einsum("nd,nf->df", second_low, pre_grad, preferred_element_type=jnp.float32)
    grad_inner, grad_outer = ffn_ready(grad_inner, grad_outer)
    second_up = third_grad + jnp.einsum(
        "nf,df->nd", pre_grad, inner_full, preferred_element_type=jnp.float32
    )
    second_grad, gain_two, bias_two = norm_back(
        second_up, second_normed, second_inverse, gain_rows[2]
    )
    second_grad_low = second_grad.astype(jnp.bfloat16)
    grad_cross_out = jnp.einsum(
        "ne,nd->ed", cross_mix, second_grad_low, preferred_element_type=jnp.float32
    )
    cross_mix_grad = jnp.einsum(
        "nd,ed->ne", second_grad_low, attn_full[7], preferred_element_type=jnp.float32
    ).astype(jnp.bfloat16)
    shaped_kv = cross_kv.reshape(2, row_count, -1, model_width)
    cross_q_grad, cross_k_grad, cross_v_grad = attend_rows_back(
        cross_query.reshape(row_count, length, model_width),
        shaped_kv[0],
        shaped_kv[1],
        cross_mix_grad.reshape(row_count, length, model_width),
        cross_lse,
        seg_tgt,
        seg_src,
        False,
    )
    cross_q_grad = cross_q_grad.reshape(-1, model_width)
    kv_grad = jnp.stack(
        [cross_k_grad.reshape(-1, model_width), cross_v_grad.reshape(-1, model_width)]
    )
    grad_cross_query = jnp.einsum(
        "nd,ne->de", first_low, cross_q_grad, preferred_element_type=jnp.float32
    )
    grad_cross_kv = jnp.einsum(
        "md,jme->jde", memory_flat, kv_grad, preferred_element_type=jnp.float32
    )
    memory_grad = jnp.einsum(
        "jme,jde->md", kv_grad, attn_full[5:7], preferred_element_type=jnp.float32
    )
    first_up = second_grad + jnp.einsum(
        "ne,de->nd", cross_q_grad, attn_full[4], preferred_element_type=jnp.float32
    )
    first_grad, gain_one, bias_one = norm_back(first_up, first_normed, first_inverse, gain_rows[0])
    first_grad_low = first_grad.astype(jnp.bfloat16)
    grad_self_out = jnp.einsum(
        "ne,nd->ed", self_mix, first_grad_low, preferred_element_type=jnp.float32
    )
    self_mix_grad = jnp.einsum(
        "nd,ed->ne", first_grad_low, attn_full[3], preferred_element_type=jnp.float32
    ).astype(jnp.bfloat16)
    shaped_self = self_proj.reshape(3, row_count, length, model_width)
    query_grad, key_grad, value_grad = attend_rows_back(
        shaped_self[0],
        shaped_self[1],
        shaped_self[2],
        self_mix_grad.reshape(row_count, length, model_width),
        self_lse,
        seg_tgt,
        seg_tgt,
        True,
    )
    qkv_grad = jnp.stack(
        [
            query_grad.reshape(-1, model_width),
            key_grad.reshape(-1, model_width),
            value_grad.reshape(-1, model_width),
        ]
    )
    grad_self_qkv = jnp.einsum(
        "nd,jne->jde", tokens_flat, qkv_grad, preferred_element_type=jnp.float32
    )
    tokens_grad = first_grad + jnp.einsum(
        "jne,jde->nd", qkv_grad, attn_full[0:3], preferred_element_type=jnp.float32
    )
    grad_attn = jnp.concatenate(
        [
            grad_self_qkv,
            grad_self_out[None],
            grad_cross_query[None],
            grad_cross_kv,
            grad_cross_out[None],
        ]
    )
    grad_norm = jnp.stack([gain_one, bias_one, gain_two, bias_two, gain_three, bias_three])
    return (
        tokens_grad.reshape(tgt.shape).astype(jnp.bfloat16),
        memory_grad.reshape(memory.shape).astype(jnp.bfloat16),
        grad_attn,
        grad_inner,
        grad_outer,
        grad_norm,
    )


def adam_direction(master, gradient, moments):
    first_moment = beta_first * moments[0] + (1.0 - beta_first) * gradient
    second_moment = beta_second * moments[1] + (1.0 - beta_second) * gradient * gradient
    first_fix = 1.0 - beta_first**STEP
    second_fix = 1.0 - beta_second**STEP
    direction = (
        first_moment / first_fix / (jnp.sqrt(second_moment / second_fix) + adam_eps)
        + decay_rate * master
    )
    return (direction, first_moment, second_moment)


def tensor_squares(attn_part, inner_part, outer_part, norm_part):
    return jnp.concatenate(
        [
            jnp.sum(attn_part * attn_part, axis=(1, 2)),
            jnp.sum(inner_part * inner_part)[None],
            jnp.sum(outer_part * outer_part)[None],
            jnp.sum(norm_part * norm_part, axis=1),
        ]
    )


def keep_whole(grad_inner, grad_outer):
    return (grad_inner, grad_outer)


def on_device(
    tgt,
    memory,
    cotangent,
    tgt_lengths,
    src_segments,
    attn_w,
    ffn_in,
    ffn_out,
    norm_params,
    attn_moments,
    in_moments,
    out_moments,
    norm_moments,
):
    low_attn = attn_w.astype(jnp.bfloat16)
    low_inner = ffn_in.astype(jnp.bfloat16)
    low_outer = ffn_out.astype(jnp.bfloat16)
    low_norm = norm_params.astype(jnp.bfloat16)
    weight_local = tensor_squares(attn_w, ffn_in, ffn_out, norm_params)
    weights = (
        lax.all_gather(low_attn, ("gx", "gy"), axis=1, tiled=True),
        lax.all_gather(low_inner, ("gx", "gy"), axis=0, tiled=True),
        lax.all_gather(low_outer, ("gx", "gy"), axis=0, tiled=True),
        lax.all_gather(low_norm, ("gx", "gy"), axis=1, tiled=True),
    )
    seg_tgt = jax.vmap(lambda row_lengths: segment_ids(row_lengths, tgt.shape[1]))(tgt_lengths)
    final_norm, saved = layer_forward(tgt, memory, weights, seg_tgt, src_segments)
    layer_out = final_norm.reshape(tgt.shape).astype(jnp.bfloat16)
    weights_back = (
        lax.all_gather(low_attn, ("gx", "gy"), axis=1, tiled=True),
        lax.all_gather(low_inner, ("gx", "gy"), axis=0, tiled=True),
        lax.all_gather(low_outer, ("gx", "gy"), axis=0, tiled=True),
        lax.all_gather(low_norm, ("gx", "gy"), axis=1, tiled=True),
    )
    saved_back = layer_forward(tgt, memory, weights_back, seg_tgt, src_segments)[1]
    tgt_grad, mem_grad, grad_attn, grad_inner, grad_outer, grad_norm = layer_backward(
        cotangent, tgt, memory, weights_back, seg_tgt, src_segments, saved_back, keep_whole
    )
    shard_attn, shard_inner, shard_outer, shard_norm = (
        lax.psum_scatter(grad_attn, ("gx", "gy"), scatter_dimension=1, tiled=True),
        lax.psum_scatter(grad_inner, ("gx", "gy"), scatter_dimension=0, tiled=True),
        lax.psum_scatter(grad_outer, ("gx", "gy"), scatter_dimension=0, tiled=True),
        lax.psum_scatter(grad_norm, ("gx", "gy"), scatter_dimension=1, tiled=True),
    )
    attn_dir, attn_first, attn_second = adam_direction(attn_w, shard_attn, attn_moments)
    inner_dir, inner_first, inner_second = adam_direction(ffn_in, shard_inner, in_moments)
    outer_dir, outer_first, outer_second = adam_direction(ffn_out, shard_outer, out_moments)
    norm_dir, norm_first, norm_second = adam_direction(norm_params, shard_norm, norm_moments)
    update_local = tensor_squares(attn_dir, inner_dir, outer_dir, norm_dir)
    weight_total, update_total = lax.psum((weight_local, update_local), ("gx", "gy"))
    ratio = jnp.sqrt(weight_total) / jnp.sqrt(update_total)
    attn_new = attn_w - learn_rate * ratio[0:8][:, None, None] * attn_dir
    in_new = ffn_in - learn_rate * ratio[8] * inner_dir
    out_new = ffn_out - learn_rate * ratio[9] * outer_dir
    norm_new = norm_params - learn_rate * ratio[10:16][:, None] * norm_dir
    norms = jnp.stack([jnp.sqrt(weight_total), jnp.sqrt(update_total)])
    return (
        layer_out,
        tgt_grad,
        mem_grad,
        attn_new,
        in_new,
        out_new,
        norm_new,
        attn_first,
        attn_second,
        inner_first,
        inner_second,
        outer_first,
        outer_second,
        norm_first,
        norm_second,
        attn_new.astype(jnp.bfloat16),
        in_new.astype(jnp.bfloat16),
        out_new.astype(jnp.bfloat16),
        norm_new.astype(jnp.bfloat16),
        norms,
    )


def solution(mesh):
    placed = (
        P(("gx", "gy"), None, None),
        P(("gx", "gy"), None, None),
        P(("gx", "gy"), None, None),
        P(("gx", "gy"), None),
        P(("gx", "gy"), None),
        P(None, ("gx", "gy"), None),
        P(("gx", "gy"), None),
        P(("gx", "gy"), None),
        P(None, ("gx", "gy")),
        P(None, None, ("gx", "gy"), None),
        P(None, ("gx", "gy"), None),
        P(None, ("gx", "gy"), None),
        P(None, None, ("gx", "gy")),
    )
    return jax.shard_map(
        on_device,
        mesh=mesh,
        in_specs=placed,
        out_specs=(
            P(("gx", "gy"), None, None),
            P(("gx", "gy"), None, None),
            P(("gx", "gy"), None, None),
            P(None, ("gx", "gy"), None),
            P(("gx", "gy"), None),
            P(("gx", "gy"), None),
            P(None, ("gx", "gy")),
            P(None, ("gx", "gy"), None),
            P(None, ("gx", "gy"), None),
            P(("gx", "gy"), None),
            P(("gx", "gy"), None),
            P(("gx", "gy"), None),
            P(("gx", "gy"), None),
            P(None, ("gx", "gy")),
            P(None, ("gx", "gy")),
            P(None, ("gx", "gy"), None),
            P(("gx", "gy"), None),
            P(("gx", "gy"), None),
            P(None, ("gx", "gy")),
            P(),
        ),
        check_vma=False,
    )
```

profile of v0, /device:TPU:10, one launch (start us, length us, event | category | flops | bytes accessed | tf_op | source)
XLA Modules:
  0.0 1141.6 jit_solution(17452787423257287904)
XLA Ops:
  15.8 33.6 %all-gather = bf16[32,16,6]{1,2,0:T(8,128)(2,1)S(1)} all-gather(bf16[1,16,6]{1,2,0:T(8,128)(2,1)S(1)} %convert_bitcast_fusion.3), channel_id=1, replica_groups=mesh['gx'=4,'gy'=8] {'gx','gy'}, dimensions={0}, use_global_device_ids=true | all-gather | bytes 6336 | tf_op jit(solution)/shard_map/all_gather | solution.py:418
  51.8 22.9 %all-gather.5.cloned.1.call-done = bf16[8,512,512]{2,0,1:T(8,128)(2,1)} async-done(((bf16[8,16,512]{2,0,1:T(8,128)(2,1)}), bf16[8,512,512]{2,0,1:T(8,128)(2,1)}) %all-gather.5.cloned.1.call-update) | async-done | bytes 4194320 | tf_op jit(solution)/shard_map/all_gather | solution.py:415
  88.6 54.7 %while.131 = (s32[]{:T(128)}, bf16[2,512,512]{2,1,0:T(8,128)(2,1)}, s32[2]{0:T(128)S(1)}, s32[1024]{0:T(1024)S(1)}, bf16[1024,512]{0,1:T(8,128)(2,1)S(1)}, /*ind...) while((s32[]{:T(128)}, bf16[2,512,512]{2,1,0:T(8,128)(2,1)}, ...), condition=%wide.region_5.6_spmd, body=%wide.region_2.5_spmd.sunk | while | flops 1100744192 | bytes 40942256 | solution.py:85
  92.1 10.5 fusion.292
  102.6 9.3 fusion.293
  119.4 10.6 fusion.292
  130.0 9.4 fusion.293
  143.3 9.4 fusion.170
  167.5 47.6 %while.132 = (s32[]{:T(128)}, bf16[2,512,512]{2,1,0:T(8,128)(2,1)}, s32[2]{0:T(128)S(1)}, s32[1024]{0:T(1024)S(1)}, s32[1024]{0:T(1024)S(1)}, /*index=5*/bf16[10...) while((s32[]{:T(128)}, bf16[2,512,512]{2,1,0:T(8,128)(2,1)}, ...), condition=%wide.region_11.12_spmd, body=%wide.region_8.11_spmd.sunk | while | flops 1099695104 | bytes 41986744 | solution.py:85
  171.3 10.4 fusion.297
  181.7 8.6 fusion.298
  195.1 10.4 fusion.297
  205.5 8.5 fusion.298
  220.4 10.7 fusion.182
  234.8 39.1 %while.133 = (s32[]{:T(128)}, bf16[2,512,512]{2,1,0:T(8,128)(2,1)}, f32[2,8,512,1]{2,1,3,0:T(8,128)S(1)}, s32[2]{0:T(128)S(1)}, s32[1024]{0:T(1024)S(1)}, /*inde...) while((s32[]{:T(128)}, bf16[2,512,512]{2,1,0:T(8,128)(2,1)}, ...), condition=%wide.region_19.20_spmd, body=%wide.region_16.19_spmd.sunk | while | flops 1125904896 | bytes 63060700 | solution.py:85
  244.8 5.8 fusion.305
  264.3 5.8 fusion.305
  284.0 33.3 %while.134 = (s32[]{:T(128)}, bf16[2,512,512]{2,1,0:T(8,128)(2,1)}, f32[2,8,512,1]{2,1,3,0:T(8,128)S(1)}, s32[2]{0:T(128)S(1)}, s32[1024]{0:T(1024)S(1)}, /*inde...) while((s32[]{:T(128)}, bf16[2,512,512]{2,1,0:T(8,128)(2,1)}, ...), condition=%wide.region_25.26_spmd, body=%wide.region_22.25_spmd.sunk | while | flops 1124855808 | bytes 63056604 | solution.py:85
  347.4 160.1 %while.135 = (s32[]{:T(128)}, f32[1024,8,64]{0,2,1:T(8,128)}, f32[1024,8,64]{0,2,1:T(8,128)}, bf16[2,512,512]{2,1,0:T(8,128)(2,1)}, s32[2]{0:T(128)S(1)}, /*inde...) while((s32[]{:T(128)}, f32[1024,8,64]{0,2,1:T(8,128)}, ...), condition=%wide.region_36.37_spmd.clone, body=%wide.region_34.36_spmd.clone.sunk | while | flops 2745968640 | bytes 144239440 | solution.py:131
  352.2 9.5 subtract_exponential_fusion.8
  361.9 8.1 fusion.322
  370.0 22.7 %fusion.323 = bf16[8,512,64]{1,2,0:T(8,128)(2,1)} fusion(bf16[1024,8,64]{0,2,1:T(8,128)(2,1)} %get-tuple-element.1741, f32[8,512,1024]{2,1,0:T(8,128)} %subtract_exponential_fusion.8, f32[8,512,1024]{2,1,0:T(8,128)} %fusion.322), kind=kOutput, calls=%fused_computation.75.clone.1 | convolution fusion | flops 558109696 | bytes 35127296 | tf_op jit(solution)/shard_map/while/body/eval_jaxpr/while/body/eval_jaxpr/hqk,khd->qhd/dot_general | solution.py:116
  394.8 23.4 %bitcast_add_fusion.9 = f32[1024,8,64]{0,2,1:T(8,128)} fusion(f32[1024,8,64]{0,2,1:T(8,128)} %get-tuple-element.1717, bf16[512,8,64]{0,2,1:T(8,128)(2,1)} %bitcast.414, f32[8,512,1024]{2,1,0:T(8,128)} %subtract_exponential_fusion.8, f32[8,512,1024]{2,1,0:T(8,128)} %fusion.322, pred[]{:T(512)S(6)} %compare.6), kind=kOutput, calls=%fused_computation.74.clone.1 | convolution fusion | flops 558896128 | bytes 38273024 | tf_op jit(solution)/shard_map/while/body/eval_jaxpr/while/body/eval_jaxpr/hqk,qhd->khd/dot_general | solution.py:119
  418.2 8.7 bitcast_add_fusion.10
  431.6 9.5 subtract_exponential_fusion.8
  441.4 8.1 fusion.322
  449.5 22.7 %fusion.323 = bf16[8,512,64]{1,2,0:T(8,128)(2,1)} fusion(bf16[1024,8,64]{0,2,1:T(8,128)(2,1)} %get-tuple-element.1741, f32[8,512,1024]{2,1,0:T(8,128)} %subtract_exponential_fusion.8, f32[8,512,1024]{2,1,0:T(8,128)} %fusion.322), kind=kOutput, calls=%fused_computation.75.clone.1 | convolution fusion | flops 558109696 | bytes 35127296 | tf_op jit(solution)/shard_map/while/body/eval_jaxpr/while/body/eval_jaxpr/hqk,khd->qhd/dot_general | solution.py:116
  474.3 24.0 %bitcast_add_fusion.9 = f32[1024,8,64]{0,2,1:T(8,128)} fusion(f32[1024,8,64]{0,2,1:T(8,128)} %get-tuple-element.1717, bf16[512,8,64]{0,2,1:T(8,128)(2,1)} %bitcast.414, f32[8,512,1024]{2,1,0:T(8,128)} %subtract_exponential_fusion.8, f32[8,512,1024]{2,1,0:T(8,128)} %fusion.322, pred[]{:T(512)S(6)} %compare.6), kind=kOutput, calls=%fused_computation.74.clone.1 | convolution fusion | flops 558896128 | bytes 38273024 | tf_op jit(solution)/shard_map/while/body/eval_jaxpr/while/body/eval_jaxpr/hqk,qhd->khd/dot_general | solution.py:119
  498.2 9.2 bitcast_add_fusion.10
  507.6 5.5 multiply_reduce_fusion.3
  514.3 6.7 fusion.152
  534.9 161.4 %while.136 = (s32[]{:T(128)}, f32[1024,8,64]{0,2,1:T(8,128)}, f32[1024,8,64]{0,2,1:T(8,128)}, bf16[2,512,512]{2,1,0:T(8,128)(2,1)}, s32[2]{0:T(128)S(1)}, /*inde...) while((s32[]{:T(128)}, f32[1024,8,64]{0,2,1:T(8,128)}, ...), condition=%wide.region_41.42_spmd.clone, body=%wide.region_39.41_spmd.clone.sunk | while | flops 2747017728 | bytes 144243536 | solution.py:131
  539.9 9.5 subtract_exponential_fusion.9
  549.6 8.1 fusion.335
  557.8 22.8 %fusion.336 = bf16[8,512,64]{1,2,0:T(8,128)(2,1)} fusion(bf16[1024,8,64]{0,2,1:T(8,128)(2,1)} %get-tuple-element.1789, f32[8,512,1024]{2,1,0:T(8,128)} %subtract_exponential_fusion.9, f32[8,512,1024]{2,1,0:T(8,128)} %fusion.335), kind=kOutput, calls=%fused_computation.100.clone.1 | convolution fusion | flops 558109696 | bytes 35127296 | tf_op jit(solution)/shard_map/while/body/eval_jaxpr/while/body/eval_jaxpr/hqk,khd->qhd/dot_general | solution.py:116
  582.7 23.5 %bitcast_add_fusion.11 = f32[1024,8,64]{0,2,1:T(8,128)} fusion(f32[1024,8,64]{0,2,1:T(8,128)} %get-tuple-element.1767, bf16[512,8,64]{0,2,1:T(8,128)(2,1)} %bitcast.416, f32[8,512,1024]{2,1,0:T(8,128)} %subtract_exponential_fusion.9, f32[8,512,1024]{2,1,0:T(8,128)} %fusion.335, pred[]{:T(512)S(6)} %compare.7), kind=kOutput, calls=%fused_computation.97.clone.1 | convolution fusion | flops 558896128 | bytes 38273024 | tf_op jit(solution)/shard_map/while/body/eval_jaxpr/while/body/eval_jaxpr/hqk,qhd->khd/dot_general | solution.py:119
  606.1 8.8 bitcast_add_fusion.12
  619.9 9.5 subtract_exponential_fusion.9
  629.6 8.1 fusion.335
  637.8 22.9 %fusion.336 = bf16[8,512,64]{1,2,0:T(8,128)(2,1)} fusion(bf16[1024,8,64]{0,2,1:T(8,128)(2,1)} %get-tuple-element.1789, f32[8,512,1024]{2,1,0:T(8,128)} %subtract_exponential_fusion.9, f32[8,512,1024]{2,1,0:T(8,128)} %fusion.335), kind=kOutput, calls=%fused_computation.100.clone.1 | convolution fusion | flops 558109696 | bytes 35127296 | tf_op jit(solution)/shard_map/while/body/eval_jaxpr/while/body/eval_jaxpr/hqk,khd->qhd/dot_general | solution.py:116
  662.7 24.2 %bitcast_add_fusion.11 = f32[1024,8,64]{0,2,1:T(8,128)} fusion(f32[1024,8,64]{0,2,1:T(8,128)} %get-tuple-element.1767, bf16[512,8,64]{0,2,1:T(8,128)(2,1)} %bitcast.416, f32[8,512,1024]{2,1,0:T(8,128)} %subtract_exponential_fusion.9, f32[8,512,1024]{2,1,0:T(8,128)} %fusion.335, pred[]{:T(512)S(6)} %compare.7), kind=kOutput, calls=%fused_computation.97.clone.1 | convolution fusion | flops 558896128 | bytes 38273024 | tf_op jit(solution)/shard_map/while/body/eval_jaxpr/while/body/eval_jaxpr/hqk,qhd->khd/dot_general | solution.py:119
  686.9 9.4 bitcast_add_fusion.12
  713.8 5.9 bitcast_dynamic-update-slice_fusion.2
  728.3 10.5 copy.297
  755.0 18.7 %reduce-scatter.9.cloned.1.call-done = f32[16,2048]{1,0:T(8,128)} async-done(((f32[512,2048]{1,0:T(8,128)}), f32[16,2048]{1,0:T(8,128)}) %reduce-scatter.9.cloned.1.call-update) | async-done | bytes 131088 | tf_op jit(solution)/shard_map/reduce_scatter | solution.py:435
  776.0 139.0 %reduce-scatter.11.cloned.1.call-done = f32[64,512]{1,0:T(8,128)} async-done(((f32[2048,512]{1,0:T(8,128)}), f32[64,512]{1,0:T(8,128)}) %reduce-scatter.11.cloned.1.call-update) | async-done | bytes 131088 | tf_op jit(solution)/shard_map/reduce_scatter | solution.py:436
  919.9 146.0 %reduce-scatter.7.cloned.1.call-done = f32[8,16,512]{2,0,1:T(8,128)} async-done(((f32[8,512,512]{2,0,1:T(8,128)}), f32[8,16,512]{2,0,1:T(8,128)}) %reduce-scatter.7.cloned.1.call-update) | async-done | bytes 262160 | tf_op jit(solution)/shard_map/reduce_scatter | solution.py:434
  1071.6 53.8 %all-reduce = (f32[16]{0:T(128)S(1)}, f32[16]{0:T(128)S(1)}) all-reduce(f32[16]{0:T(128)S(1)} %pad_maximum_fusion.8, f32[16]{0:T(128)S(1)} %copy-done.114), channel_id=1, replica_groups=mesh['gx'=4,'gy'=8] {'gx','gy'}, use_global_device_ids=true, to_apply=%region_61.62 | all-reduce | flops 32 | bytes 256 | tf_op jit(solution)/shard_map/psum | solution.py:444
  (495 shorter events, 263.1 us)
Async XLA Ops:
  7.2 153.8 %copy-start = (bf16[1,1024,512]{2,1,0:T(8,128)(2,1)S(1)}, bf16[1,1024,512]{2,1,0:T(8,128)(2,1)}, u32[]{:S(2)}) copy-start(bf16[1,1024,512]{2,1,0:T(8,128)(2,1)} %param.26) | copy-start | bytes 3145732
  7.2 43.1 %copy-start.48 = (bf16[1,1024,512]{2,1,0:T(8,128)(2,1)S(1)}, bf16[1,1024,512]{2,1,0:T(8,128)(2,1)}, u32[]{:S(2)}) copy-start(bf16[1,1024,512]{2,1,0:T(8,128)(2,1)} %param.27) | copy-start | bytes 3145732
  7.2 67.5 %all-gather.5.cloned.1.call-start = ((), (), s32[]{:S(2)}) async-start(), calls=%async_computation.4 | async-start | bytes 4325376 | tf_op jit(solution)/shard_map/all_gather | solution.py:415
  9.2 211.2 %all-gather.7.cloned.1.call-start = ((), (), s32[]{:S(2)}) async-start(), calls=%async_computation.5 | async-start | bytes 2162688 | tf_op jit(solution)/shard_map/all_gather | solution.py:416
  10.8 209.6 %all-gather.9.cloned.1.call-start = ((), (), s32[]{:S(2)}) async-start(), calls=%async_computation.6 | async-start | bytes 2162688 | tf_op jit(solution)/shard_map/all_gather | solution.py:417
  12.4 741.1 %reduce-scatter.13.cloned.1.call-start = ((), (), s32[]{:S(2)}) async-start(), calls=%async_computation.10 | async-start | bytes 270336
  50.3 164.9 %copy-start.80 = (f32[1,512]{1,0:T(1,128)}, f32[1,512]{1,0:T(1,128)S(1)}, u32[]{:S(2)}) copy-start(f32[1,512]{1,0:T(1,128)S(1)} %get-tuple-element.1176) | copy-start | bytes 6148
  50.3 164.9 %copy-start.107 = (f32[1,512]{1,0:T(1,128)}, f32[1,512]{1,0:T(1,128)S(1)}, u32[]{:S(2)}) copy-start(f32[1,512]{1,0:T(1,128)S(1)} %get-tuple-element.1175) | copy-start | bytes 6148
  50.9 27.9 %copy-start.23 = (bf16[1,1024,512]{1,2,0:T(8,128)(2,1)}, bf16[1,1024,512]{1,2,0:T(8,128)(2,1)S(1)}, u32[]{:S(2)}) copy-start(bf16[1,1024,512]{1,2,0:T(8,128)(2,1)S(1)} %copy.275) | copy-start | bytes 3145732
  143.3 9.4 copy-start.6
  143.3 9.4 copy-start.26
  143.3 9.4 copy-start.41
  284.0 33.3 %copy-start.65 = (f32[1024]{0:T(1024)S(1)}, f32[1024]{0:T(1024)}, u32[]{:S(2)}) copy-start(f32[1024]{0:T(1024)} %copy-done.64) | copy-start | bytes 12292
  284.0 33.3 %copy-start.75 = (f32[1024]{0:T(1024)S(1)}, f32[1024]{0:T(1024)}, u32[]{:S(2)}) copy-start(f32[1024]{0:T(1024)} %copy-done.74) | copy-start | bytes 12292
  284.0 33.3 %copy-start.82 = (f32[1,512]{1,0:T(1,128)S(1)}, f32[1,512]{1,0:T(1,128)}, u32[]{:S(2)}) copy-start(f32[1,512]{1,0:T(1,128)} %copy-done.80) | copy-start | bytes 6148
  284.0 33.3 %copy-start.109 = (f32[1,512]{1,0:T(1,128)S(1)}, f32[1,512]{1,0:T(1,128)}, u32[]{:S(2)}) copy-start(f32[1,512]{1,0:T(1,128)} %copy-done.107) | copy-start | bytes 6148
  320.5 22.8 %copy-start.31 = (f32[1024,512]{0,1:T(8,128)}, f32[1024,512]{0,1:T(8,128)S(1)}, u32[]{:S(2)}) copy-start(f32[1024,512]{0,1:T(8,128)S(1)} %get-tuple-element.1188) | copy-start | bytes 6291460
  320.6 22.8 %copy-start.78 = (f32[1024]{0:T(1024)}, f32[1024]{0:T(1024)S(1)}, u32[]{:S(2)}) copy-start(f32[1024]{0:T(1024)S(1)} %broadcast_multiply_fusion.7) | copy-start | bytes 12292
  322.9 20.4 %copy-start.90 = (f32[1024]{0:T(1024)}, f32[1024]{0:T(1024)S(1)}, u32[]{:S(2)}) copy-start(f32[1024]{0:T(1024)S(1)} %add_rsqrt_fusion.1) | copy-start | bytes 12292
  329.5 9.7 copy-start.28
  329.5 9.7 copy-start.68
  347.4 160.1 %copy-start.66 = (f32[1024]{0:T(1024)S(1)}, f32[1024]{0:T(1024)}, u32[]{:S(2)}) copy-start(f32[1024]{0:T(1024)} %copy-done.64) | copy-start | bytes 12292
  347.4 160.1 %copy-start.76 = (f32[1024]{0:T(1024)S(1)}, f32[1024]{0:T(1024)}, u32[]{:S(2)}) copy-start(f32[1024]{0:T(1024)} %copy-done.74) | copy-start | bytes 12292
  347.4 160.1 %copy-start.83 = (f32[1,512]{1,0:T(1,128)S(1)}, f32[1,512]{1,0:T(1,128)}, u32[]{:S(2)}) copy-start(f32[1,512]{1,0:T(1,128)} %copy-done.80) | copy-start | bytes 6148
  350.2 11.5 %copy-start.19 = (bf16[512,512]{0,1:T(8,128)(2,1)}, bf16[512,512]{0,1:T(8,128)(2,1)S(1)}, u32[]{:S(2)}) copy-start(bf16[512,512]{0,1:T(8,128)(2,1)S(1)} %constant_dynamic-slice_fusion.20) | copy-start | bytes 1572868 | tf_op jit(solution)/shard_map/while/body/eval_jaxpr/while
  352.2 9.5 copy-start.22
  429.7 11.4 %copy-start.19 = (bf16[512,512]{0,1:T(8,128)(2,1)}, bf16[512,512]{0,1:T(8,128)(2,1)S(1)}, u32[]{:S(2)}) copy-start(bf16[512,512]{0,1:T(8,128)(2,1)S(1)} %constant_dynamic-slice_fusion.20) | copy-start | bytes 1572868 | tf_op jit(solution)/shard_map/while/body/eval_jaxpr/while
  431.6 9.5 copy-start.22
  514.0 259.8 %reduce-scatter.9.cloned.1.call-start = ((), (), s32[]{:S(2)}) async-start(), calls=%async_computation.8 | async-start | bytes 4325376 | tf_op jit(solution)/shard_map/reduce_scatter | solution.py:435
  521.1 394.0 %reduce-scatter.11.cloned.1.call-start = ((), (), s32[]{:S(2)}) async-start(), calls=%async_computation.9 | async-start | bytes 4325376 | tf_op jit(solution)/shard_map/reduce_scatter | solution.py:436
  533.4 532.5 %reduce-scatter.7.cloned.1.call-start = ((), (), s32[]{:S(2)}) async-start(), calls=%async_computation.7 | async-start | bytes 8650752 | tf_op jit(solution)/shard_map/reduce_scatter | solution.py:434
  537.9 11.5 %copy-start.20 = (bf16[512,512]{0,1:T(8,128)(2,1)}, bf16[512,512]{0,1:T(8,128)(2,1)S(1)}, u32[]{:S(2)}) copy-start(bf16[512,512]{0,1:T(8,128)(2,1)S(1)} %constant_dynamic-slice_fusion.22) | copy-start | bytes 1572868 | tf_op jit(solution)/shard_map/while/body/eval_jaxpr/while
  539.9 9.5 copy-start.21
  617.9 11.5 %copy-start.20 = (bf16[512,512]{0,1:T(8,128)(2,1)}, bf16[512,512]{0,1:T(8,128)(2,1)S(1)}, u32[]{:S(2)}) copy-start(bf16[512,512]{0,1:T(8,128)(2,1)S(1)} %constant_dynamic-slice_fusion.22) | copy-start | bytes 1572868 | tf_op jit(solution)/shard_map/while/body/eval_jaxpr/while
  619.9 9.5 copy-start.21
  749.3 24.5 %copy-start.47 = (f32[16,2048]{1,0:T(8,128)S(1)}, f32[16,2048]{1,0:T(8,128)}, u32[]{:S(2)}) copy-start(f32[16,2048]{1,0:T(8,128)} %param.31) | copy-start | bytes 393220
  749.3 24.5 %copy-start.62 = (f32[2,16,2048]{2,1,0:T(8,128)S(1)}, f32[2,16,2048]{2,1,0:T(8,128)}, u32[]{:S(2)}) copy-start(f32[2,16,2048]{2,1,0:T(8,128)} %param.35) | copy-start | bytes 786436
  749.3 165.8 %copy-start.46 = (f32[64,512]{1,0:T(8,128)S(1)}, f32[64,512]{1,0:T(8,128)}, u32[]{:S(2)}) copy-start(f32[64,512]{1,0:T(8,128)} %param.32) | copy-start | bytes 393220
  749.3 165.8 %copy-start.63 = (f32[2,64,512]{2,1,0:T(8,128)S(1)}, f32[2,64,512]{2,1,0:T(8,128)}, u32[]{:S(2)}) copy-start(f32[2,64,512]{2,1,0:T(8,128)} %param.36) | copy-start | bytes 786436
  749.3 316.6 %copy-start.53 = (f32[1,8,16,512]{3,2,1,0:T(8,128)S(1)}, f32[1,8,16,512]{3,2,1,0:T(8,128)}, u32[]{:S(2)}) copy-start(f32[1,8,16,512]{3,2,1,0:T(8,128)} %get-tuple-element.1169) | copy-start | bytes 786436
  753.5 316.7 %copy-start.37 = (bf16[1,1024,512]{1,2,0:T(8,128)(2,1)S(1)}, bf16[1,1024,512]{1,2,0:T(8,128)(2,1)}, u32[]{:S(2)}) copy-start(bf16[1,1024,512]{1,2,0:T(8,128)(2,1)} %get-tuple-element.1179) | copy-start | bytes 3145732
  755.0 377.3 %copy-start.88 = (f32[6,16]{1,0:T(8,128)}, f32[6,16]{1,0:T(8,128)S(1)}, u32[]{:S(2)}) copy-start(f32[6,16]{1,0:T(8,128)S(1)} %get-tuple-element.1151) | copy-start | bytes 1156
  755.0 377.3 %copy-start.89 = (f32[6,16]{1,0:T(8,128)}, f32[6,16]{1,0:T(8,128)S(1)}, u32[]{:S(2)}) copy-start(f32[6,16]{1,0:T(8,128)S(1)} %get-tuple-element.1152) | copy-start | bytes 1156
  776.0 357.8 %copy-start.56 = (f32[16,2048]{1,0:T(8,128)}, f32[16,2048]{1,0:T(8,128)S(1)}, u32[]{:S(2)}) copy-start(f32[16,2048]{1,0:T(8,128)S(1)} %get-tuple-element.1147) | copy-start | bytes 393220
  919.9 151.7 %copy-start.114 = (f32[16]{0:T(128)S(1)}, f32[16]{0:T(128)}, u32[]{:S(2)}) copy-start(f32[16]{0:T(128)} %pad_maximum_fusion.7) | copy-start | bytes 196
  1071.6 61.5 %copy-start.58 = (f32[64,512]{1,0:T(8,128)S(1)}, f32[64,512]{1,0:T(8,128)}, u32[]{:S(2)}) copy-start(f32[64,512]{1,0:T(8,128)} %get-tuple-element.1149) | copy-start | bytes 393220
  1071.6 61.5 %copy-start.59 = (f32[64,512]{1,0:T(8,128)S(1)}, f32[64,512]{1,0:T(8,128)}, u32[]{:S(2)}) copy-start(f32[64,512]{1,0:T(8,128)} %get-tuple-element.1150) | copy-start | bytes 393220
  1071.6 62.2 %copy-start.57 = (f32[16,2048]{1,0:T(8,128)S(1)}, f32[16,2048]{1,0:T(8,128)}, u32[]{:S(2)}) copy-start(f32[16,2048]{1,0:T(8,128)} %get-tuple-element.1148) | copy-start | bytes 393220
  (85 other events, 264.3 us)
Sparse Core Ops, SparseCore 0:
  11.6 63.0 all-gather.4
  78.2 54.3 all-gather.6
  136.2 55.3 all-gather.8
  514.1 118.4 reduce-scatter.12
  634.8 138.8 reduce-scatter.8
  776.0 139.0 reduce-scatter.10
  917.5 148.3 reduce-scatter.6
where the time goes:
time: 1150 us; the launch traced here: 1140 us
  matrix products  493 us (43%)
  waiting for transfers between devices  327 us (28%)
  local copies, waits for them, and re-layouts  137 us (12%)
  blocking collectives  87.5 us (8%)
  other arithmetic  62.4 us (5%)
  loops' own time  17.2 us (1%)
  between operations  16.8 us (1%)
    reduce_scatter x1, waiting for transfers between devices, on_device(): lax.psum_scatter(grad_attn, ('gx', 'gy'), scatter_dimension=1, tiled=True)  146 us
    reduce_scatter x1, waiting for transfers between devices, on_device(): lax.psum_scatter(grad_outer, ('gx', 'gy'), scatter_dimension=0, tiled=True)  139 us
    dot_general x4, matrix products, one_block(): jnp.einsum('hqk,qhd->khd', grad_score, query_block, preferred_element_typ...  95 us
    dot_general x4, matrix products, one_block(): jnp.einsum('hqk,khd->qhd', grad_score, key_heads, preferred_element_type=...  91.1 us
    dot_general x8, matrix products, one_block(): jnp.einsum('hqk,khd->qhd', probability, value_heads, preferred_element_ty...  57.6 us
    psum x1, blocking collectives, on_device(): lax.psum((weight_local, update_local), ('gx', 'gy'))  53.8 us
    dot_general x8, matrix products, block_logits(): jnp.einsum('qhd,khd->hqk', query_block, key_heads, preferred_element_type...  50 us
    sub x4, matrix products, one_block(): exponent = jnp.exp(logits - row_max)  41.9 us
  transfers between devices with their start and end apart: 7, of which 4 were waited for; matrix products, arithmetic and copies ran while one was open for 34% of the time, Pallas kernels for 0%

commit v1 on v0

v1 whole, which is shorter than its diff:
```python
import functools

import jax
import jax.numpy as jnp
from jax import lax
from jax.experimental import pallas as pl
from jax.experimental.pallas import tpu as pltpu
from jax.sharding import PartitionSpec as P

HEAD_DIM = 64
STEP = 5

beta_first = 0.5
beta_second = 0.5
learn_rate = 0.5
decay_rate = 0.01
norm_eps = 1e-05
adam_eps = 1e-06

f32 = jnp.float32
bf16 = jnp.bfloat16
LANES = 128
QB = 128
KB = 256
RC = 256
MASKED = -1e30
AXES = ("gx", "gy")
MIB = 2**20


def nn(left, right):
    return lax.dot_general(left, right, (((1,), (0,)), ((), ())), preferred_element_type=f32)


def nt(left, right):
    return lax.dot_general(left, right, (((1,), (1,)), ((), ())), preferred_element_type=f32)


def tn(left, right):
    return lax.dot_general(left, right, (((0,), (0,)), ((), ())), preferred_element_type=f32)


def rows_of(step, size):
    return pl.ds(pl.multiple_of(step * size, size), size)


def each_chunk(count, body):
    def step(index, carry):
        body(index)
        return carry

    lax.fori_loop(0, count, step, 0)


def spread_heads(dst, src):
    pairs = dst.shape[0]
    first = lax.broadcasted_iota(jnp.int32, (QB, LANES), 1) < HEAD_DIM
    zero = jnp.zeros((QB, LANES), bf16)

    def body(i):
        start = pl.multiple_of(i * 2 * QB, 2 * QB)
        for p in range(pairs):
            tile = src[rows_of(i, QB), p * LANES : (p + 1) * LANES]
            dst[p, pl.ds(start, QB), :] = jnp.where(first, tile, zero)
            dst[p, pl.ds(start + QB, QB), :] = jnp.where(first, zero, tile)

    each_chunk(src.shape[0] // QB, body)


def key_block(first_key, j, keys):
    nominal = first_key * LANES + j * KB
    return pl.multiple_of(jnp.minimum(nominal, keys - KB), LANES), nominal


def block_bias(low, high, start, nominal):
    place = start + lax.broadcasted_iota(jnp.int32, (KB, QB), 0)
    bias = jnp.where((place >= jnp.maximum(low, nominal)) & (place < high), 0.0, MASKED).astype(f32)
    return jnp.concatenate([bias, bias], axis=1)


def attention(spans, which, bounds, key_ref, value_t, query_z, mixed_ref, lse_ref, score_scr, out_scr):
    keys = key_ref.shape[0]
    pairs = query_z.shape[0]
    fold = (KB // 8, 8, 2 * QB)

    def query_block(i):
        rows = rows_of(i, QB)
        pair_rows = rows_of(i, 2 * QB)
        low = bounds[2 * which : 2 * which + 1, rows]
        high = bounds[2 * which + 1 : 2 * which + 2, rows]
        first_key = spans[2 * which, i]
        blocks = spans[2 * which + 1, i]
        out_scr[...] = jnp.zeros_like(out_scr)

        def scores(j, tops):
            start, nominal = key_block(first_key, j, keys)
            bias = block_bias(low, high, start, nominal)
            found = []
            for p in range(pairs):
                lanes = slice(p * LANES, (p + 1) * LANES)
                score = nt(key_ref[pl.ds(start, KB), lanes], query_z[p, pair_rows, :]) + bias
                score_scr[p, rows_of(j, KB), :] = score
                found.append(jnp.maximum(tops[p], jnp.max(score.reshape(fold), axis=0)))
            return tuple(found)

        tops = lax.fori_loop(
            0, blocks, scores, tuple(jnp.full((8, 2 * QB), MASKED, f32) for _ in range(pairs))
        )
        top = [jnp.max(t, axis=0, keepdims=True) for t in tops]

        def weigh(j, sums):
            start, _ = key_block(first_key, j, keys)
            found = []
            for p in range(pairs):
                exponent = jnp.exp(score_scr[p, rows_of(j, KB), :] - top[p])
                found.append(sums[p] + jnp.sum(exponent.reshape(fold), axis=0))
                low_exp = exponent.astype(bf16)
                for h in range(2):
                    heads = slice(h * HEAD_DIM, (h + 1) * HEAD_DIM)
                    value = value_t[
                        p * LANES + h * HEAD_DIM : p * LANES + (h + 1) * HEAD_DIM, pl.ds(start, KB)
                    ]
                    out_scr[p, heads, :] += nn(value, low_exp[:, h * QB : (h + 1) * QB])
            return tuple(found)

        sums = lax.fori_loop(
            0, blocks, weigh, tuple(jnp.zeros((8, 2 * QB), f32) for _ in range(pairs))
        )
        for p in range(pairs):
            total = jnp.sum(sums[p], axis=0, keepdims=True)
            lse_ref[i, p : p + 1, :] = top[p] + jnp.log(total)
            inverse = 1.0 / total
            out = jnp.concatenate(
                [out_scr[p, 0:HEAD_DIM, :] * inverse[:, :QB], out_scr[p, HEAD_DIM:, :] * inverse[:, QB:]],
                axis=0,
            )
            mixed_ref[rows, p * LANES : (p + 1) * LANES] = out.T.astype(bf16)

    each_chunk(query_z.shape[1] // (2 * QB), query_block)


def attention_back(
    spans, which, bounds, key_ref, key_t, value_ref, query_z, grad_z, grad_ref, mixed_ref, lse_ref,
    dquery_ref, dkey_scr, dvalue_scr, dq_scr,
):
    keys = key_ref.shape[0]
    pairs = query_z.shape[0]

    def query_block(i):
        rows = rows_of(i, QB)
        pair_rows = rows_of(i, 2 * QB)
        low = bounds[2 * which : 2 * which + 1, rows]
        high = bounds[2 * which + 1 : 2 * which + 2, rows]
        first_key = spans[2 * which, i]
        blocks = spans[2 * which + 1, i]
        dq_scr[...] = jnp.zeros_like(dq_scr)
        deltas = []
        for p in range(pairs):
            lanes = slice(p * LANES, (p + 1) * LANES)
            product = (grad_ref[rows, lanes].astype(f32) * mixed_ref[rows, lanes].astype(f32)).T
            deltas.append(
                jnp.concatenate(
                    [
                        jnp.sum(product[:HEAD_DIM], axis=0, keepdims=True),
                        jnp.sum(product[HEAD_DIM:], axis=0, keepdims=True),
                    ],
                    axis=1,
                )
            )

        def key_step(j):
            start, nominal = key_block(first_key, j, keys)
            bias = block_bias(low, high, start, nominal)
            block = pl.ds(start, KB)
            for p in range(pairs):
                lanes = slice(p * LANES, (p + 1) * LANES)
                query = query_z[p, pair_rows, :]
                grad = grad_z[p, pair_rows, :]
                score = nt(key_ref[block, lanes], query)
                dprob = nt(value_ref[block, lanes], grad)
                prob = jnp.exp(score + bias - lse_ref[i, p : p + 1, :])
                dscore = (prob * (dprob - deltas[p])).astype(bf16)
                dvalue_scr[block, lanes] += nn(prob.astype(bf16), grad)
                dkey_scr[block, lanes] += nn(dscore, query)
                for h in range(2):
                    heads = slice(h * HEAD_DIM, (h + 1) * HEAD_DIM)
                    key = key_t[
                        p * LANES + h * HEAD_DIM : p * LANES + (h + 1) * HEAD_DIM, block
                    ]
                    dq_scr[p, heads, :] += nn(key, dscore[:, h * QB : (h + 1) * QB])

        each_chunk(blocks, key_step)
        for p in range(pairs):
            dquery_ref[rows, p * LANES : (p + 1) * LANES] = (
                (dq_scr[p] * HEAD_DIM**-0.5).T.astype(bf16)
            )

    each_chunk(query_z.shape[1] // (2 * QB), query_block)


def norm_parts(values):
    average = jnp.mean(values, axis=-1, keepdims=True)
    centred = values - average
    spread = jnp.mean(centred * centred, axis=-1, keepdims=True)
    inverse = lax.rsqrt(spread + norm_eps)
    return centred * inverse, inverse


def norm_back(gradient, normed, inverse, gain):
    scaled = gradient * gain
    first_mean = jnp.mean(scaled, axis=-1, keepdims=True)
    second_mean = jnp.mean(scaled * normed, axis=-1, keepdims=True)
    return inverse * (scaled - first_mean - normed * second_mean)


def fold_rows(values):
    return jnp.sum(values.reshape(values.shape[0] // 8, 8, values.shape[1]), axis=0)


def forward_kernel(
    spans, bounds, tgt, memory, attn, norm,
    q_ref, k_ref, v_ref, mix_ref, lse_ref, cq_ref, ck_ref, cv_ref, cmix_ref, clse_ref,
    n1_ref, s1_ref, n2_ref, s2_ref,
    query_z, value_t, score_scr, out_scr, h1_scr,
):
    chunks = tgt.shape[0] // RC
    scale = jnp.array(HEAD_DIM**-0.5, bf16)

    def project(c):
        rows = rows_of(c, RC)
        x = tgt[rows, :]
        q_ref[rows, :] = nn(x, attn[0]).astype(bf16) * scale
        k_ref[rows, :] = nn(x, attn[1]).astype(bf16)
        v_ref[rows, :] = nn(x, attn[2]).astype(bf16)

    each_chunk(chunks, project)
    spread_heads(query_z, q_ref)
    value_t[...] = v_ref[...].T
    attention(spans, 0, bounds, k_ref, value_t, query_z, mix_ref, lse_ref, score_scr, out_scr)

    def middle(c):
        rows = rows_of(c, RC)
        normed, inverse = norm_parts(tgt[rows, :].astype(f32) + nn(mix_ref[rows, :], attn[3]))
        n1_ref[rows, :] = normed
        s1_ref[rows, :] = inverse
        h1 = normed * norm[0:1, :].astype(f32) + norm[1:2, :].astype(f32)
        h1_scr[rows, :] = h1
        cq_ref[rows, :] = nn(h1.astype(bf16), attn[4]).astype(bf16) * scale
        mem = memory[rows, :]
        ck_ref[rows, :] = nn(mem, attn[5]).astype(bf16)
        cv_ref[rows, :] = nn(mem, attn[6]).astype(bf16)

    each_chunk(chunks, middle)
    spread_heads(query_z, cq_ref)
    value_t[...] = cv_ref[...].T
    attention(spans, 1, bounds, ck_ref, value_t, query_z, cmix_ref, clse_ref, score_scr, out_scr)

    def last(c):
        rows = rows_of(c, RC)
        normed, inverse = norm_parts(h1_scr[rows, :] + nn(cmix_ref[rows, :], attn[7]))
        n2_ref[rows, :] = normed
        s2_ref[rows, :] = inverse

    each_chunk(chunks, last)


def ffn_kernel(
    n2_ref, s2_ref, cot_ref, inner, outer, norm,
    out_ref, d2_ref, ginner_ref, gouter_ref, gnorm_ref,
    h2_scr, act_scr, d3_scr, dpre_scr, sums,
):
    chunks = n2_ref.shape[0] // RC
    hidden = inner.shape[1]
    sums[...] = jnp.zeros_like(sums)

    def body(c):
        rows = rows_of(c, RC)
        n2 = n2_ref[rows, :]
        h2 = n2 * norm[2:3, :].astype(f32) + norm[3:4, :].astype(f32)
        h2b = h2.astype(bf16)
        h2_scr[rows, :] = h2b
        pre = nn(h2b, inner[...])
        sig = 1.0 / (1.0 + jnp.exp(-pre))
        act = (pre * sig).astype(bf16)
        act_scr[rows, :] = act
        n3, s3 = norm_parts(h2 + nn(act, outer[...]))
        out_ref[rows, :] = (n3 * norm[4:5, :].astype(f32) + norm[5:6, :].astype(f32)).astype(bf16)
        cot = cot_ref[rows, :].astype(f32)
        sums[2] += fold_rows(cot * n3)
        sums[3] += fold_rows(cot)
        d3 = norm_back(cot, n3, s3, norm[4:5, :].astype(f32))
        d3b = d3.astype(bf16)
        d3_scr[rows, :] = d3b
        dpre = (nt(d3b, outer[...]) * (sig * (1.0 + pre * (1.0 - sig)))).astype(bf16)
        dpre_scr[rows, :] = dpre
        dh2 = d3 + nt(dpre, inner[...])
        sums[0] += fold_rows(dh2 * n2)
        sums[1] += fold_rows(dh2)
        d2_ref[rows, :] = norm_back(dh2, n2, s2_ref[rows, :], norm[2:3, :].astype(f32))

    each_chunk(chunks, body)
    for i in range(4):
        gnorm_ref[i : i + 1, :] = jnp.sum(sums[i], axis=0, keepdims=True)
    part = 2 * RC

    def grads(c):
        cols = rows_of(c, part)
        gouter_ref[cols, :] = tn(act_scr[:, cols], d3_scr[...]).astype(bf16)
        ginner_ref[:, cols] = tn(h2_scr[...], dpre_scr[:, cols]).astype(bf16)

    each_chunk(hidden // part, grads)


def cross_back_kernel(
    spans, bounds, d2_ref, memory, cq_ref, ck_ref, cv_ref, cmix_ref, clse_ref, n1_ref, s1_ref, attn, norm,
    d1_ref, mgrad_ref, gattn_ref, gnorm_ref,
    query_z, grad_z, key_t, grad_scr, dq_scr, dk_scr, dv_scr, acc_scr, h1_scr, sums,
):
    chunks = d2_ref.shape[0] // RC
    sums[...] = jnp.zeros_like(sums)

    def enter(c):
        rows = rows_of(c, RC)
        d2b = d2_ref[rows, :].astype(bf16)
        h1_scr[rows, :] = d2b
        grad_scr[rows, :] = nt(d2b, attn[7]).astype(bf16)

    each_chunk(chunks, enter)
    gattn_ref[3] = tn(cmix_ref[...], h1_scr[...]).astype(bf16)
    spread_heads(query_z, cq_ref)
    spread_heads(grad_z, grad_scr)
    key_t[...] = ck_ref[...].T
    dk_scr[...] = jnp.zeros_like(dk_scr)
    dv_scr[...] = jnp.zeros_like(dv_scr)
    attention_back(
        spans, 1, bounds, ck_ref, key_t, cv_ref, query_z, grad_z, grad_scr, cmix_ref, clse_ref,
        dq_scr, dk_scr, dv_scr, acc_scr,
    )

    def leave(c):
        rows = rows_of(c, RC)
        mgrad_ref[rows, :] = (
            nt(dk_scr[rows, :].astype(bf16), attn[5]) + nt(dv_scr[rows, :].astype(bf16), attn[6])
        ).astype(bf16)
        n1 = n1_ref[rows, :]
        h1_scr[rows, :] = (n1 * norm[0:1, :].astype(f32) + norm[1:2, :].astype(f32)).astype(bf16)
        dh1 = d2_ref[rows, :] + nt(dq_scr[rows, :], attn[4])
        sums[0] += fold_rows(dh1 * n1)
        sums[1] += fold_rows(dh1)
        d1_ref[rows, :] = norm_back(dh1, n1, s1_ref[rows, :], norm[0:1, :].astype(f32))

    each_chunk(chunks, leave)
    for i in range(2):
        gnorm_ref[i : i + 1, :] = jnp.sum(sums[i], axis=0, keepdims=True)
    gattn_ref[0] = tn(h1_scr[...], dq_scr[...]).astype(bf16)
    gattn_ref[1] = tn(memory[...], dk_scr[...].astype(bf16)).astype(bf16)
    gattn_ref[2] = tn(memory[...], dv_scr[...].astype(bf16)).astype(bf16)


def self_back_kernel(
    spans, bounds, d1_ref, tgt, q_ref, k_ref, v_ref, mix_ref, lse_ref, attn,
    tgrad_ref, gattn_ref,
    query_z, grad_z, key_t, grad_scr, dq_scr, dk_scr, dv_scr, acc_scr, d1_scr,
):
    chunks = d1_ref.shape[0] // RC

    def enter(c):
        rows = rows_of(c, RC)
        d1b = d1_ref[rows, :].astype(bf16)
        d1_scr[rows, :] = d1b
        grad_scr[rows, :] = nt(d1b, attn[3]).astype(bf16)

    each_chunk(chunks, enter)
    gattn_ref[3] = tn(mix_ref[...], d1_scr[...]).astype(bf16)
    spread_heads(query_z, q_ref)
    spread_heads(grad_z, grad_scr)
    key_t[...] = k_ref[...].T
    dk_scr[...] = jnp.zeros_like(dk_scr)
    dv_scr[...] = jnp.zeros_like(dv_scr)
    attention_back(
        spans, 0, bounds, k_ref, key_t, v_ref, query_z, grad_z, grad_scr, mix_ref, lse_ref,
        dq_scr, dk_scr, dv_scr, acc_scr,
    )

    def leave(c):
        rows = rows_of(c, RC)
        tgrad_ref[rows, :] = (
            d1_ref[rows, :]
            + nt(dq_scr[rows, :], attn[0])
            + nt(dk_scr[rows, :].astype(bf16), attn[1])
            + nt(dv_scr[rows, :].astype(bf16), attn[2])
        ).astype(bf16)

    each_chunk(chunks, leave)
    gattn_ref[0] = tn(tgt[...], dq_scr[...]).astype(bf16)
    gattn_ref[1] = tn(tgt[...], dk_scr[...].astype(bf16)).astype(bf16)
    gattn_ref[2] = tn(tgt[...], dv_scr[...].astype(bf16)).astype(bf16)


def shape(dims, dtype):
    return jax.ShapeDtypeStruct(dims, dtype)


def call(kernel, outs, scratch, scalars, args):
    smem = pl.BlockSpec(memory_space=pltpu.SMEM)
    vmem = pl.BlockSpec(memory_space=pltpu.VMEM)
    return pl.pallas_call(
        kernel,
        out_shape=outs,
        in_specs=[smem] * scalars + [vmem] * (len(args) - scalars),
        out_specs=tuple(vmem for _ in outs),
        scratch_shapes=[pltpu.VMEM(dims, dtype) for dims, dtype in scratch],
        compiler_params=pltpu.CompilerParams(vmem_limit_bytes=56 * MIB),
    )(*args)


def segment_bounds(lengths, src_segments, length):
    sentences = lengths.shape[0]
    ends = jnp.cumsum(lengths)
    starts = ends - lengths
    sizes = jnp.sum(
        (src_segments[None, :] == jnp.arange(sentences, dtype=jnp.int32)[:, None]).astype(jnp.int32), axis=1
    )
    places = jnp.arange(length, dtype=jnp.int32)
    ended = ends[:, None] <= places[None, :]
    begun = starts[:, None] <= places[None, :]
    self_low = jnp.sum(jnp.where(ended, lengths[:, None], 0), axis=0)
    cross_low = jnp.sum(jnp.where(ended, sizes[:, None], 0), axis=0)
    cross_high = jnp.sum(jnp.where(begun, sizes[:, None], 0), axis=0)
    bounds = jnp.stack([self_low, places + 1, cross_low, cross_high]).astype(jnp.int32)
    firsts = bounds[0::2, 0::QB] // LANES
    lasts = (bounds[1::2, QB - 1 :: QB] + LANES - 1) // LANES
    counts = ((lasts - firsts) * LANES + KB - 1) // KB
    spans = jnp.stack([firsts[0], counts[0], firsts[1], counts[1]]).astype(jnp.int32)
    return bounds, spans


def layer(tgt, memory, cotangent, lengths, src_segments, attn, inner, outer, norm):
    length, width = tgt.shape
    keys = memory.shape[0]
    hidden = inner.shape[1]
    pairs = width // LANES
    blocks = length // QB
    bounds, spans = segment_bounds(lengths, src_segments, length)
    row = (length, width)
    mem_row = (keys, width)
    lse = (blocks, pairs, 2 * QB)
    most = max(length, keys)
    zeroed = ((pairs, 2 * length, LANES), bf16)
    (q, k, v, mix, row_lse, cq, ck, cv, cmix, cross_lse, n1, s1, n2, s2) = call(
        forward_kernel,
        (
            shape(row, bf16), shape(row, bf16), shape(row, bf16), shape(row, bf16), shape(lse, f32),
            shape(row, bf16), shape(mem_row, bf16), shape(mem_row, bf16), shape(row, bf16), shape(lse, f32),
            shape(row, f32), shape((length, 1), f32), shape(row, f32), shape((length, 1), f32),
        ),
        [
            zeroed,
            ((width, most), bf16),
            ((pairs, most + KB, 2 * QB), f32),
            ((pairs, LANES, QB), f32),
            (row, f32),
        ],
        1,
        (spans, bounds, tgt, memory, attn, norm),
    )
    layer_out, d2, grad_inner, grad_outer, norm_late = call(
        ffn_kernel,
        (
            shape(row, bf16), shape(row, f32), shape((width, hidden), bf16), shape((hidden, width), bf16),
            shape((4, width), f32),
        ),
        [(row, bf16), ((length, hidden), bf16), (row, bf16), ((length, hidden), bf16), ((4, 8, width), f32)],
        0,
        (n2, s2, cotangent, inner, outer, norm),
    )
    back_scratch = [
        zeroed, zeroed, ((width, most), bf16), (row, bf16), (row, bf16), (mem_row, f32), (mem_row, f32),
        ((pairs, LANES, QB), f32), (row, bf16),
    ]
    d1, mem_grad, grad_cross, norm_early = call(
        cross_back_kernel,
        (shape(row, f32), shape(mem_row, bf16), shape((4, width, width), bf16), shape((2, width), f32)),
        back_scratch + [((2, 8, width), f32)],
        1,
        (spans, bounds, d2, memory, cq, ck, cv, cmix, cross_lse, n1, s1, attn, norm),
    )
    tgt_grad, grad_self = call(
        self_back_kernel,
        (shape(row, bf16), shape((4, width, width), bf16)),
        back_scratch,
        1,
        (spans, bounds, d1, tgt, q, k, v, mix, row_lse, attn),
    )
    grad_norm = jnp.concatenate([norm_early, norm_late])
    return layer_out, tgt_grad, mem_grad, grad_self, grad_cross, grad_inner, grad_outer, grad_norm


def adam_direction(master, gradient, moments):
    first_moment = beta_first * moments[0] + (1.0 - beta_first) * gradient
    second_moment = beta_second * moments[1] + (1.0 - beta_second) * gradient * gradient
    first_fix = 1.0 - beta_first**STEP
    second_fix = 1.0 - beta_second**STEP
    direction = (
        first_moment / first_fix / (jnp.sqrt(second_moment / second_fix) + adam_eps)
        + decay_rate * master
    )
    return (direction, first_moment, second_moment)


def tensor_squares(attn_part, inner_part, outer_part, norm_part):
    return jnp.concatenate(
        [
            jnp.sum(attn_part * attn_part, axis=(1, 2)),
            jnp.sum(inner_part * inner_part)[None],
            jnp.sum(outer_part * outer_part)[None],
            jnp.sum(norm_part * norm_part, axis=1),
        ]
    )


def on_device(
    tgt, memory, cotangent, tgt_lengths, src_segments, attn_w, ffn_in, ffn_out, norm_params,
    attn_moments, in_moments, out_moments, norm_moments,
):
    weight_local = tensor_squares(attn_w, ffn_in, ffn_out, norm_params)
    attn = lax.all_gather(attn_w.astype(bf16), AXES, axis=1, tiled=True)
    inner = lax.all_gather(ffn_in.astype(bf16), AXES, axis=0, tiled=True)
    outer = lax.all_gather(ffn_out.astype(bf16), AXES, axis=0, tiled=True)
    norm = lax.all_gather(norm_params.astype(bf16), AXES, axis=1, tiled=True)
    rows = tgt.shape[0]
    parts = [
        layer(tgt[r], memory[r], cotangent[r], tgt_lengths[r], src_segments[r], attn, inner, outer, norm)
        for r in range(rows)
    ]
    layer_out, tgt_grad, mem_grad = (jnp.stack([part[i] for part in parts]) for i in range(3))
    grads = [sum(part[i].astype(f32) for part in parts) for i in range(3, 8)]
    grad_attn = jnp.concatenate([grads[0], grads[1]]).astype(bf16)
    shard_attn = lax.psum_scatter(grad_attn, AXES, scatter_dimension=1, tiled=True).astype(f32)
    shard_inner = lax.psum_scatter(grads[2].astype(bf16), AXES, scatter_dimension=0, tiled=True).astype(f32)
    shard_outer = lax.psum_scatter(grads[3].astype(bf16), AXES, scatter_dimension=0, tiled=True).astype(f32)
    shard_norm = lax.psum_scatter(grads[4], AXES, scatter_dimension=1, tiled=True)
    attn_dir, attn_first, attn_second = adam_direction(attn_w, shard_attn, attn_moments)
    inner_dir, inner_first, inner_second = adam_direction(ffn_in, shard_inner, in_moments)
    outer_dir, outer_first, outer_second = adam_direction(ffn_out, shard_outer, out_moments)
    norm_dir, norm_first, norm_second = adam_direction(norm_params, shard_norm, norm_moments)
    update_local = tensor_squares(attn_dir, inner_dir, outer_dir, norm_dir)
    weight_total, update_total = lax.psum((weight_local, update_local), AXES)
    ratio = jnp.sqrt(weight_total) / jnp.sqrt(update_total)
    attn_new = attn_w - learn_rate * ratio[0:8][:, None, None] * attn_dir
    in_new = ffn_in - learn_rate * ratio[8] * inner_dir
    out_new = ffn_out - learn_rate * ratio[9] * outer_dir
    norm_new = norm_params - learn_rate * ratio[10:16][:, None] * norm_dir
    norms = jnp.stack([jnp.sqrt(weight_total), jnp.sqrt(update_total)])
    return (
        layer_out, tgt_grad, mem_grad, attn_new, in_new, out_new, norm_new,
        attn_first, attn_second, inner_first, inner_second, outer_first, outer_second, norm_first, norm_second,
        attn_new.astype(bf16), in_new.astype(bf16), out_new.astype(bf16), norm_new.astype(bf16), norms,
    )


def solution(mesh):
    rows = P(AXES, None, None)
    matrix = P(AXES, None)
    stack = P(None, AXES, None)
    vectors = P(None, AXES)
    return jax.shard_map(
        on_device,
        mesh=mesh,
        in_specs=(
            rows, rows, rows, matrix, matrix, stack, matrix, matrix, vectors,
            P(None, None, AXES, None), stack, stack, P(None, None, AXES),
        ),
        out_specs=(
            rows, rows, rows, stack, matrix, matrix, vectors, stack, stack, matrix, matrix, matrix, matrix,
            vectors, vectors, stack, matrix, matrix, vectors, P(),
        ),
        check_vma=False,
    )
```

time: 1150 us -> 852 us (0.74); the launches traced: 1140 us -> 855 us
  matrix products: 493 us -> 0 us
  waiting for transfers between devices: 327 us -> 609 us
  local copies, waits for them, and re-layouts: 137 us -> 4.6 us
  Pallas kernels: 0 us -> 115 us
  other arithmetic: 62.4 us -> 24.1 us
  loops' own time: 17.2 us -> 0 us
    dot_general x57 -> x0, matrix products: 451 us -> none  [the longest x4 95 us: one_block(): jnp.einsum('hqk,qhd->khd', grad_score, query_block, preferred_element_typ...]
    pallas_call x0 -> x4, Pallas kernels: none -> 115 us  [call(): pl.pallas_call(kernel, out_shape=outs, in_specs=[smem] * scalars + [vmem]...]
    reduce_scatter x3, waiting for transfers between devices: 304 us -> 408 us  [the longest x1 140 us: on_device(): lax.psum_scatter(grad_attn, AXES, scatter_dimension=1, tiled=True)]
    unnamed x8, waiting for transfers between devices: 0.12 us -> 94.4 us
    all_gather x3, waiting for transfers between devices: 22.9 us -> 107 us  [the longest x1 58.9 us: on_device(): outer = lax.all_gather(ffn_out.astype(bf16), AXES, axis=0, tiled=True)]
    sub x4 -> x0, matrix products: 41.9 us -> none  [one_block(): exponent = jnp.exp(logits - row_max)]
    unnamed x241 -> x41, local copies, waits for them, and re-layouts: 35.7 us -> 3.05 us
    dynamic_update_slice x24 -> x0, local copies, waits for them, and re-layouts: 28.2 us -> none  [attend_row(): mixture, log_sums = lax.map(one_block, jnp.arange(length // block_rows))]
  transfers between devices with their start and end apart: 7 -> 7, of which waited for: 4 -> 7; matrix products, arithmetic and copies ran while one was open for 34% -> 2% of each run, Pallas kernels for 0% -> 7%
where the time goes in v1:
time: 852 us; the launch traced here: 855 us
  waiting for transfers between devices  609 us (71%)
  Pallas kernels  115 us (13%)
  blocking collectives  86.6 us (10%)
  other arithmetic  24.1 us (3%)
  between operations  15.6 us (2%)
    reduce_scatter x1, waiting for transfers between devices, on_device(): lax.psum_scatter(grad_attn, AXES, scatter_dimension=1, tiled=True)  140 us
    reduce_scatter x1, waiting for transfers between devices, on_device(): lax.psum_scatter(grads[2].astype(bf16), AXES, scatter_dimension=0, tiled=...  134 us
    reduce_scatter x1, waiting for transfers between devices, on_device(): lax.psum_scatter(grads[3].astype(bf16), AXES, scatter_dimension=0, tiled=...  134 us
    pallas_call x4, Pallas kernels, call(): pl.pallas_call(kernel, out_shape=outs, in_specs=[smem] * scalars + [vmem]...  115 us
    unnamed x8, waiting for transfers between devices  94.4 us
    all_gather x1, waiting for transfers between devices, on_device(): outer = lax.all_gather(ffn_out.astype(bf16), AXES, axis=0, tiled=True)  58.9 us
    psum x1, blocking collectives, on_device(): weight_total, update_total = lax.psum((weight_local, update_local), AXES)  53 us
    all_gather x1, blocking collectives, on_device(): norm = lax.all_gather(norm_params.astype(bf16), AXES, axis=1, tiled=True)  33.6 us
  transfers between devices with their start and end apart: 7, of which 7 were waited for; matrix products, arithmetic and copies ran while one was open for 2% of the time, Pallas kernels for 7%

profile of v1, /device:TPU:10, one launch (start us, length us, event | category | flops | bytes accessed | tf_op | source)
XLA Modules:
  0.0 855.4 jit_solution(4525499367147886341)
XLA Ops:
  7.2 1.6 convert_element_type.44
  8.9 1.5 convert_element_type.46
  10.6 1.5 convert_element_type.47
  12.2 0.7 copy.45
  12.9 0.1 reduce-window.7
  13.0 0.1 reduce
  13.1 0.8 convert_reduce_fusion
  13.9 0.7 bitcast_subtract_fusion
  14.6 0.8 select_reduce_fusion.2
  15.4 0.1 slice.54
  15.5 0.1 slice.56
  15.6 0.7 convert_bitcast_fusion
  16.3 33.6 %all-gather = bf16[32,16,6]{1,2,0:T(8,128)(2,1)S(1)} all-gather(bf16[1,16,6]{1,2,0:T(8,128)(2,1)S(1)} %convert_bitcast_fusion), channel_id=1, replica_groups=mesh['gx'=4,'gy'=8] {'gx','gy'}, dimensions={0}, use_global_device_ids=true | all-gather | bytes 6336 | tf_op jit(solution)/shard_map/all_gather | solution.py:530
  50.0 0.7 reshape.101
  50.7 0.6 pad_add_fusion.1.spans
  51.3 23.4 %all-gather.5.cloned.1.call-done.attn = bf16[8,512,512]{2,1,0:T(8,128)(2,1)} async-done(((bf16[8,16,512]{2,1,0:T(8,128)(2,1)}), bf16[8,512,512]{2,1,0:T(8,128)(2,1)}) %all-gather.5.cloned.1.call-update) | async-done | bytes 4194320 | tf_op jit(solution)/shard_map/all_gather | solution.py:527
  74.7 33.1 %shard_map.284 = (bf16[1024,512]{1,0:T(8,128)(2,1)}, bf16[1024,512]{1,0:T(8,128)(2,1)}, bf16[1024,512]{1,0:T(8,128)(2,1)}, bf16[1024,512]{1,0:T(8,128)(2,1)}, f3...) custom-call(s32[4,8]{1,0:T(4,128)} %pad_add_fusion.1.spans, ...), custom_call_target="tpu_custom_call" | custom-call | tf_op jit(solution)/shard_map/pallas_call | solution.py:407
  107.8 24.4 %all-gather.7.cloned.1.call-done.inner = bf16[512,2048]{1,0:T(8,128)(2,1)} async-done(((bf16[16,2048]{1,0:T(8,128)(2,1)}), bf16[512,2048]{1,0:T(8,128)(2,1)}) %all-gather.7.cloned.1.call-update) | async-done | bytes 2097168 | tf_op jit(solution)/shard_map/all_gather | solution.py:528
  132.3 58.9 %all-gather.9.cloned.1.call-done.outer = bf16[2048,512]{1,0:T(8,128)(2,1)} async-done(((bf16[64,512]{1,0:T(8,128)(2,1)}), bf16[2048,512]{1,0:T(8,128)(2,1)}) %all-gather.9.cloned.1.call-update) | async-done | bytes 2097168 | tf_op jit(solution)/shard_map/all_gather | solution.py:529
  191.2 23.1 %shard_map.285 = (bf16[1024,512]{1,0:T(8,128)(2,1)}, f32[1024,512]{1,0:T(8,128)}, bf16[512,2048]{1,0:T(8,128)(2,1)}, bf16[2048,512]{1,0:T(8,128)(2,1)}, f32[4,512]{1,0:T(4,128)}) custom-call(f32[1024,512]{1,0:T(8,128)} %get-tuple-element.45.n2_ref, f32[1024,1]{1,0:T(8,128)} %get-tuple-element.46.s2_ref, bf16[1024,512]{1,0:T(8,128)(2,1)} %bitcast.64, ...), custom_call_target="tpu_custom_call" | custom-call | tf_op jit(solution)/shard_map/pallas_call | solution.py:407
  214.3 28.7 %shard_map.286 = (f32[1024,512]{1,0:T(8,128)}, bf16[1024,512]{1,0:T(8,128)(2,1)}, bf16[4,512,512]{2,1,0:T(8,128)(2,1)}, f32[2,512]{1,0:T(2,128)}) custom-call(s32[4,8]{1,0:T(4,128)} %pad_add_fusion.1.spans, s32[4,1024]{1,0:T(4,128)} %copy-done.11, f32[1024,512]{1,0:T(8,128)} %get-tuple-element.48.d2_ref, bf16[1024,512]{1,0:T(8,128)(2,1)} %bitcast.63, ...), custom_call_target="tpu_custom_call" | custom-call | tf_op jit(solution)/shard_map/pallas_call | solution.py:407
  243.0 0.7 pad_maximum_fusion.1
  243.7 0.9 copy.49
  244.6 0.5 reduce-scatter.9.cloned.1.call-update
  245.2 0.2 reduce-scatter.11.cloned.1.call-start
  245.4 0.3 reduce-scatter.11.cloned.1.call-update
  245.8 29.8 %shard_map.287 = (bf16[1024,512]{1,0:T(8,128)(2,1)}, bf16[4,512,512]{2,1,0:T(8,128)(2,1)}) custom-call(s32[4,8]{1,0:T(4,128)} %pad_add_fusion.1.spans, s32[4,1024]{1,0:T(4,128)} %copy-done.11, f32[1024,512]{1,0:T(8,128)} %get-tuple-element.56.d1_ref, bf16[1024,512]{1,0:T(8,128)(2,1)} %bitcast.61, bf16[1024,512]{1,0:T(8,128)(2,1)} %get-tuple-element.57.q_ref, ...), custom_call_target="tpu_custom_call" | custom-call | tf_op jit(solution)/shard_map/pallas_call | solution.py:407
  275.6 3.9 pad_maximum_fusion
  279.6 0.6 copy-done.18
  280.2 93.5 %reduce-scatter.13.cloned.1.call-done = f32[16,6]{1,0:T(8,128)} async-done(((f32[512,6]{1,0:T(8,128)}), f32[16,6]{1,0:T(8,128)}) %reduce-scatter.13.cloned.1.call-update) | async-done | bytes 400
  373.7 0.8 copy.50
  374.5 0.1 multiply_reduce_fusion.7
  374.6 134.2 %reduce-scatter.9.cloned.1.call-done = bf16[16,2048]{1,0:T(8,128)(2,1)} async-done(((bf16[512,2048]{1,0:T(8,128)(2,1)}), bf16[16,2048]{1,0:T(8,128)(2,1)}) %reduce-scatter.9.cloned.1.call-update) | async-done | bytes 65552 | tf_op jit(solution)/shard_map/reduce_scatter | solution.py:540
  508.9 1.6 multiply_reduce_fusion.5
  510.4 134.0 %reduce-scatter.11.cloned.1.call-done = bf16[64,512]{1,0:T(8,128)(2,1)} async-done(((bf16[2048,512]{1,0:T(8,128)(2,1)}), bf16[64,512]{1,0:T(8,128)(2,1)}) %reduce-scatter.11.cloned.1.call-update) | async-done | bytes 65552 | tf_op jit(solution)/shard_map/reduce_scatter | solution.py:541
  644.4 1.6 multiply_reduce_fusion.4
  646.0 139.9 %reduce-scatter.7.cloned.1.call-done = bf16[8,16,512]{2,1,0:T(8,128)(2,1)} async-done(((bf16[8,512,512]{2,1,0:T(8,128)(2,1)}), bf16[8,16,512]{2,1,0:T(8,128)(2,1)}) %reduce-scatter.7.cloned.1.call-update) | async-done | bytes 131088 | tf_op jit(solution)/shard_map/reduce_scatter | solution.py:539
  785.9 1.2 multiply_reduce_fusion.1
  787.1 1.4 pad_maximum_fusion.3
  788.5 1.4 pad_maximum_fusion.4
  789.9 53.0 %all-reduce = (f32[16]{0:T(128)S(1)}, f32[16]{0:T(128)S(1)}) all-reduce(f32[16]{0:T(128)S(1)} %pad_maximum_fusion.4, f32[16]{0:T(128)S(1)} %pad_maximum_fusion.3), channel_id=1, replica_groups=mesh['gx'=4,'gy'=8] {'gx','gy'}, use_global_device_ids=true, to_apply=%region_18.19 | all-reduce | flops 32 | bytes 256 | tf_op jit(solution)/shard_map/psum | solution.py:548
  842.8 0.1 slice_multiply_fusion
  842.9 0.6 fusion.17
  844.8 0.6 pad_maximum_fusion.2
  845.4 0.7 fusion.6
  846.0 0.8 fusion.7
  846.8 0.8 fusion.8
  847.5 0.9 fusion.9
  (56 shorter events, 0.5 us)
Async XLA Ops:
  7.2 67.5 %all-gather.5.cloned.1.call-start = ((), (), s32[]{:S(2)}) async-start(), calls=%async_computation.4 | async-start | bytes 4325376 | tf_op jit(solution)/shard_map/all_gather | solution.py:527
  8.9 123.4 %all-gather.7.cloned.1.call-start = ((), (), s32[]{:S(2)}) async-start(), calls=%async_computation.5 | async-start | bytes 2162688 | tf_op jit(solution)/shard_map/all_gather | solution.py:528
  10.5 180.7 %all-gather.9.cloned.1.call-start = ((), (), s32[]{:S(2)}) async-start(), calls=%async_computation.6 | async-start | bytes 2162688 | tf_op jit(solution)/shard_map/all_gather | solution.py:529
  12.1 361.6 %reduce-scatter.13.cloned.1.call-start = ((), (), s32[]{:S(2)}) async-start(), calls=%async_computation.10 | async-start | bytes 270336
  15.4 59.3 %copy-start.11 = (s32[4,1024]{1,0:T(4,128)}, s32[4,1024]{1,0:T(4,128)S(1)}, u32[]{:S(2)}) copy-start(s32[4,1024]{1,0:T(4,128)S(1)} %pad_add_fusion.bounds) | copy-start | bytes 49156
  214.3 28.7 %copy-start.17 = (f32[4,512]{1,0:T(4,128)S(1)}, f32[4,512]{1,0:T(4,128)}, u32[]{:S(2)}) copy-start(f32[4,512]{1,0:T(4,128)} %get-tuple-element.69) | copy-start | bytes 24580
  244.6 264.3 %reduce-scatter.9.cloned.1.call-start = ((), (), s32[]{:S(2)}) async-start(), calls=%async_computation.8 | async-start | bytes 2162688 | tf_op jit(solution)/shard_map/reduce_scatter | solution.py:540
  245.2 399.2 %reduce-scatter.11.cloned.1.call-start = ((), (), s32[]{:S(2)}) async-start(), calls=%async_computation.9 | async-start | bytes 2162688 | tf_op jit(solution)/shard_map/reduce_scatter | solution.py:541
  245.8 540.1 %reduce-scatter.7.cloned.1.call-start = ((), (), s32[]{:S(2)}) async-start(), calls=%async_computation.7 | async-start | bytes 4325376 | tf_op jit(solution)/shard_map/reduce_scatter | solution.py:539
  245.8 29.8 %copy-start.1 = (bf16[4,512,512]{2,1,0:T(8,128)(2,1)S(1)}, bf16[4,512,512]{2,1,0:T(8,128)(2,1)}, u32[]{:S(2)}) copy-start(bf16[4,512,512]{2,1,0:T(8,128)(2,1)} %get-tuple-element.65) | copy-start | bytes 6291460
  279.5 0.7 copy-start.18
  279.5 94.9 %copy-start.14 = (f32[6,16]{1,0:T(8,128)S(1)}, f32[6,16]{1,0:T(8,128)}, u32[]{:S(2)}) copy-start(f32[6,16]{1,0:T(8,128)} %param.21) | copy-start | bytes 1156
  279.5 229.3 %copy-start.3 = (f32[16,2048]{1,0:T(8,128)S(1)}, f32[16,2048]{1,0:T(8,128)}, u32[]{:S(2)}) copy-start(f32[16,2048]{1,0:T(8,128)} %param.19) | copy-start | bytes 393220
  279.5 229.3 %copy-start.12 = (f32[2,16,2048]{2,1,0:T(8,128)S(1)}, f32[2,16,2048]{2,1,0:T(8,128)}, u32[]{:S(2)}) copy-start(f32[2,16,2048]{2,1,0:T(8,128)} %param.23) | copy-start | bytes 786436
  279.5 364.9 %copy-start.2 = (f32[64,512]{1,0:T(8,128)S(1)}, f32[64,512]{1,0:T(8,128)}, u32[]{:S(2)}) copy-start(f32[64,512]{1,0:T(8,128)} %param.20) | copy-start | bytes 393220
  279.5 364.9 %copy-start.13 = (f32[2,64,512]{2,1,0:T(8,128)S(1)}, f32[2,64,512]{2,1,0:T(8,128)}, u32[]{:S(2)}) copy-start(f32[2,64,512]{2,1,0:T(8,128)} %param.24) | copy-start | bytes 786436
  279.5 506.3 %copy-start = (f32[8,16,512]{2,1,0:T(8,128)S(1)}, f32[8,16,512]{2,1,0:T(8,128)}, u32[]{:S(2)}) copy-start(f32[8,16,512]{2,1,0:T(8,128)} %param.18) | copy-start | bytes 786436
  279.6 506.3 %copy-start.6 = (f32[2,8,16,512]{3,2,1,0:T(8,128)S(1)}, f32[2,8,16,512]{3,2,1,0:T(8,128)}, u32[]{:S(2)}) copy-start(f32[2,8,16,512]{3,2,1,0:T(8,128)} %param.22) | copy-start | bytes 1572868
  374.6 473.9 %copy-start.15 = (f32[6,16]{1,0:T(8,128)}, f32[6,16]{1,0:T(8,128)S(1)}, u32[]{:S(2)}) copy-start(f32[6,16]{1,0:T(8,128)S(1)} %get-tuple-element.97) | copy-start | bytes 1156
  374.6 473.8 %copy-start.16 = (f32[6,16]{1,0:T(8,128)}, f32[6,16]{1,0:T(8,128)S(1)}, u32[]{:S(2)}) copy-start(f32[6,16]{1,0:T(8,128)S(1)} %get-tuple-element.98) | copy-start | bytes 1156
  510.4 338.0 %copy-start.7 = (f32[16,2048]{1,0:T(8,128)}, f32[16,2048]{1,0:T(8,128)S(1)}, u32[]{:S(2)}) copy-start(f32[16,2048]{1,0:T(8,128)S(1)} %get-tuple-element.93) | copy-start | bytes 393220
  510.4 338.0 %copy-start.8 = (f32[16,2048]{1,0:T(8,128)}, f32[16,2048]{1,0:T(8,128)S(1)}, u32[]{:S(2)}) copy-start(f32[16,2048]{1,0:T(8,128)S(1)} %get-tuple-element.94) | copy-start | bytes 393220
  646.0 202.5 %copy-start.9 = (f32[64,512]{1,0:T(8,128)}, f32[64,512]{1,0:T(8,128)S(1)}, u32[]{:S(2)}) copy-start(f32[64,512]{1,0:T(8,128)S(1)} %get-tuple-element.95) | copy-start | bytes 393220
  646.0 202.5 %copy-start.10 = (f32[64,512]{1,0:T(8,128)}, f32[64,512]{1,0:T(8,128)S(1)}, u32[]{:S(2)}) copy-start(f32[64,512]{1,0:T(8,128)S(1)} %get-tuple-element.96) | copy-start | bytes 393220
  787.1 61.4 %copy-start.4 = (f32[8,16,512]{2,1,0:T(8,128)}, f32[8,16,512]{2,1,0:T(8,128)S(1)}, u32[]{:S(2)}) copy-start(f32[8,16,512]{2,1,0:T(8,128)S(1)} %get-tuple-element.91) | copy-start | bytes 786436
  787.1 61.4 %copy-start.5 = (f32[8,16,512]{2,1,0:T(8,128)}, f32[8,16,512]{2,1,0:T(8,128)S(1)}, u32[]{:S(2)}) copy-start(f32[8,16,512]{2,1,0:T(8,128)S(1)} %get-tuple-element.92) | copy-start | bytes 786436
Sparse Core Ops, SparseCore 0:
  11.7 63.0 all-gather.4
  78.3 53.9 all-gather.6
  135.8 55.3 all-gather.8
  244.7 128.9 reduce-scatter.12
  375.9 132.9 reduce-scatter.8
  511.0 133.3 reduce-scatter.10
  646.8 139.0 reduce-scatter.6
